TPU v7x, 32 devices: a whole 2x2x4 slice. The times are simulated.
32 devices in a mesh: dp: 4 (over y, x), seq: 8 (over z, core).
Axes of the slice: x: 2, y: 2, z: 4, core: 2. Of those that a mesh axis runs over, the one named last changes fastest.
Arguments:
- inputs: float32 [4, 4096, 1024], P('dp', 'seq'), may hold values from -6 to 6
- norm_gain: bfloat16 [2, 1024], P(None, 'dp'), may hold values from 0.25 to 1.75
- in_weight: bfloat16 [2, 1024, 4384], P(None, 'dp'), may hold values from -0.1875 to 0.1875
- conv_weight: bfloat16 [2, 4, 2304], P(None, None, 'dp'), may hold values from -3 to 3
- conv_bias: bfloat16 [2, 2304], P(None, 'dp'), may hold values from -0.5 to 0.5
- dt_bias: bfloat16 [2, 32], P(None, 'dp'), may hold values from -6 to 0.5
- a_log: bfloat16 [2, 32], P(None, 'dp'), may hold values from -4 to 1
- skip_gain: bfloat16 [2, 32], P(None, 'dp'), may hold values from 0.5 to 2
- gate_gain: bfloat16 [2, 2048], P(None, 'dp'), may hold values from 0.25 to 1.75
- out_weight: bfloat16 [2, 2048, 1024], P(None, 'dp'), may hold values from -0.125 to 0.125
- cotangent: float32 [4, 4096, 1024], P('dp', 'seq'), may hold values from -6 to 6
Outputs:
- output: float32 [4, 4096, 1024], P('dp', 'seq')
- input_grad: float32 [4, 4096, 1024], P('dp', 'seq')
- grad_norm_gain: float32 [2, 1024], P(None, 'dp')
- grad_in_weight: float32 [2, 1024, 4384], P(None, 'dp')
- grad_conv_weight: float32 [2, 4, 2304], P(None, None, 'dp')
- grad_conv_bias: float32 [2, 2304], P(None, 'dp')
- grad_dt_bias: float32 [2, 32], P(None, 'dp')
- grad_a_log: float32 [2, 32], P(None, 'dp')
- grad_skip_gain: float32 [2, 32], P(None, 'dp')
- grad_gate_gain: float32 [2, 2048], P(None, 'dp')
- grad_out_weight: float32 [2, 2048, 1024], P(None, 'dp')
All inputs are finite; a program needn't handle non-finite values.
Results may differ from a plain program's by a relative error of at most 0.02.
Values may be sent and summed in bfloat16 or wider, within the bound.
A program may use at most 320 MiB of HBM per device.

v0:
```python
import jax
import jax.numpy as jnp
from jax import lax
from jax.sharding import PartitionSpec as P

HEADS = 32
HEAD_DIM = 64
STATE = 128
GROUP = 256
INNER = 2048
XBC = 2304


epsilon = 1e-05
highest = lax.Precision.HIGHEST


def passed_along(value, axis, steps):
    count = lax.axis_size(axis)
    first, last = (max(0, -steps), min(count, count - steps))
    return lax.ppermute(value, axis, [(source, source + steps) for source in range(first, last)])


def rms_norm(values, gain):
    return values * lax.rsqrt(jnp.mean(values * values, axis=-1, keepdims=True) + epsilon) * gain


def conv_apply(extended, conv_weight, conv_bias, length):
    total = conv_bias + jnp.zeros((length, conv_bias.shape[0]), jnp.float32)
    for tap_idx in range(conv_weight.shape[0]):
        total = total + conv_weight[tap_idx] * extended[tap_idx : tap_idx + length].astype(
            jnp.float32
        )
    return total


def shard_scan(conv_out, dt_raw, dt_bias, a_log):
    length = conv_out.shape[0]
    blocks = length // GROUP
    active = jax.nn.silu(conv_out)
    values = active[:, :INNER].reshape(blocks, GROUP, HEADS, HEAD_DIM)
    b_mat = active[:, INNER : INNER + STATE].reshape(blocks, GROUP, STATE)
    c_mat = active[:, INNER + STATE :].reshape(blocks, GROUP, STATE)
    step_size = jax.nn.softplus(dt_raw + dt_bias)
    log_decay = step_size * -jnp.exp(a_log)
    group_sum = jnp.cumsum(log_decay.reshape(blocks, GROUP, HEADS), axis=1)
    by_head = jnp.swapaxes(group_sum, 1, 2)
    causal = lax.broadcasted_iota(jnp.int32, (GROUP, GROUP), 0) >= lax.broadcasted_iota(
        jnp.int32, (GROUP, GROUP), 1
    )
    decays = jnp.exp(jnp.where(causal, by_head[:, :, :, None] - by_head[:, :, None, :], -jnp.inf))
    scores = jnp.einsum("kin,kjn->kij", c_mat, b_mat, precision=highest)
    scaled = values * step_size.reshape(blocks, GROUP, HEADS)[:, :, :, None]
    within = jnp.einsum("khij,kjhp->kihp", decays * scores[:, None], scaled, precision=highest)
    tails = jnp.exp(group_sum[:, -1:, :] - group_sum)
    group_states = jnp.einsum(
        "kjhp,kjn->khpn", scaled * tails[:, :, :, None], b_mat, precision=highest
    )
    group_decay = jnp.exp(group_sum[:, -1, :])
    running = jnp.zeros((HEADS, HEAD_DIM, STATE), jnp.float32)
    entering = []
    for block_idx in range(blocks):
        entering.append(running)
        running = group_decay[block_idx][:, None, None] * running + group_states[block_idx]
    carried = jnp.einsum("kin,khpn->kihp", c_mat, jnp.stack(entering), precision=highest)
    shard_out = within + jnp.exp(group_sum)[:, :, :, None] * carried
    shard_sum = jnp.cumsum(log_decay, axis=0)
    return (
        shard_out.reshape(length, INNER),
        running,
        jnp.exp(shard_sum[-1]),
        shard_sum,
        c_mat.reshape(length, STATE),
        values.reshape(length, INNER),
    )


def finish(shard_out, shard_sum, c_mat, values, incoming, gate_z, skip_gain, gate_gain):
    length = shard_out.shape[0]
    from_state = jnp.exp(shard_sum)[:, :, None] * jnp.einsum(
        "tn,hpn->thp", c_mat, incoming, precision=highest
    )
    skipped = skip_gain[:, None] * values.reshape(length, HEADS, HEAD_DIM)
    mixed = shard_out + (from_state + skipped).reshape(length, INNER)
    return rms_norm(mixed * jax.nn.silu(gate_z), gate_gain)


def pass_states(shard_decay, local_state):

    def advance(turn_idx, arriving):
        return passed_along(shard_decay[:, None, None] * arriving + local_state, "seq", 1)

    return lax.fori_loop(0, lax.axis_size("seq") - 1, advance, jnp.zeros_like(local_state))


def pass_back(shard_decay, direct_grad):

    def retreat(turn_idx, arriving):
        return passed_along(
            (shard_decay[:, None, None] * arriving + direct_grad).astype(jnp.bfloat16), "seq", -1
        ).astype(jnp.float32)

    return lax.fori_loop(0, lax.axis_size("seq") - 1, retreat, jnp.zeros_like(direct_grad))


def body(
    inputs,
    norm_gain,
    in_weight,
    conv_weight,
    conv_bias,
    dt_bias,
    a_log,
    skip_gain,
    gate_gain,
    out_weight,
    cotangent,
):
    layers = in_weight.shape[0]
    hidden = inputs[0]
    length = hidden.shape[0]
    rim_rows = conv_weight.shape[1] - 1
    saved = []
    for layer_idx in range(layers):
        shards = (
            norm_gain[layer_idx],
            in_weight[layer_idx],
            conv_weight[layer_idx],
            conv_bias[layer_idx],
            dt_bias[layer_idx],
            a_log[layer_idx],
            skip_gain[layer_idx],
            gate_gain[layer_idx],
            out_weight[layer_idx],
        )
        gathered = (
            lax.all_gather(shards[0], "dp", axis=0, tiled=True),
            lax.all_gather(shards[1], "dp", axis=0, tiled=True),
            lax.all_gather(shards[2], "dp", axis=1, tiled=True),
            lax.all_gather(shards[3], "dp", axis=0, tiled=True),
            lax.all_gather(shards[4], "dp", axis=0, tiled=True),
            lax.all_gather(shards[5], "dp", axis=0, tiled=True),
            lax.all_gather(shards[6], "dp", axis=0, tiled=True),
            lax.all_gather(shards[7], "dp", axis=0, tiled=True),
            lax.all_gather(shards[8], "dp", axis=0, tiled=True),
        )
        normed = rms_norm(hidden, gathered[0].astype(jnp.float32))
        normed_low = normed.astype(jnp.bfloat16)
        projected = jnp.dot(normed_low, gathered[1], preferred_element_type=jnp.float32)
        gate_z = projected[:, :INNER]
        conv_in = projected[:, INNER : INNER + XBC].astype(jnp.bfloat16)
        dt_raw = projected[:, INNER + XBC :]
        arrived = passed_along(conv_in[length - rim_rows :], "seq", 1)
        extended = jnp.concatenate([arrived, conv_in], axis=0)
        conv_out = conv_apply(
            extended, gathered[2].astype(jnp.float32), gathered[3].astype(jnp.float32), length
        )
        scanned = shard_scan(
            conv_out, dt_raw, gathered[4].astype(jnp.float32), gathered[5].astype(jnp.float32)
        )
        incoming = pass_states(scanned[2], scanned[1])
        normed_out = finish(
            scanned[0],
            scanned[3],
            scanned[4],
            scanned[5],
            incoming,
            gate_z,
            gathered[6].astype(jnp.float32),
            gathered[7].astype(jnp.float32),
        )
        branch = jnp.dot(
            normed_out.astype(jnp.bfloat16), gathered[8], preferred_element_type=jnp.float32
        )
        weight_store = shards
        saved.append(
            (hidden, normed_low, gate_z, dt_raw, extended, conv_out, incoming, weight_store)
        )
        hidden = hidden + branch
    grad_hidden = cotangent[0]
    reduced = [None] * layers
    for layer_idx in reversed(range(layers)):
        hidden_in, normed_low, gate_z, dt_raw, extended, conv_out, incoming, weight_store = saved[
            layer_idx
        ]
        gathered = (
            lax.all_gather(weight_store[0], "dp", axis=0, tiled=True),
            lax.all_gather(weight_store[1], "dp", axis=0, tiled=True),
            lax.all_gather(weight_store[2], "dp", axis=1, tiled=True),
            lax.all_gather(weight_store[3], "dp", axis=0, tiled=True),
            lax.all_gather(weight_store[4], "dp", axis=0, tiled=True),
            lax.all_gather(weight_store[5], "dp", axis=0, tiled=True),
            lax.all_gather(weight_store[6], "dp", axis=0, tiled=True),
            lax.all_gather(weight_store[7], "dp", axis=0, tiled=True),
            lax.all_gather(weight_store[8], "dp", axis=0, tiled=True),
        )
        grad_branch = grad_hidden.astype(jnp.bfloat16)
        scanned, scan_pull = jax.vjp(
            shard_scan,
            conv_out,
            dt_raw,
            gathered[4].astype(jnp.float32),
            gathered[5].astype(jnp.float32),
        )
        normed_out, finish_pull = jax.vjp(
            finish,
            scanned[0],
            scanned[3],
            scanned[4],
            scanned[5],
            incoming,
            gate_z,
            gathered[6].astype(jnp.float32),
            gathered[7].astype(jnp.float32),
        )
        low_out = normed_out.astype(jnp.bfloat16)
        grad_out_weight = lax.dot_general(
            low_out, grad_branch, (((0,), (0,)), ((), ())), preferred_element_type=jnp.float32
        )
        grad_normed_out = lax.dot_general(
            grad_branch, gathered[8], (((1,), (1,)), ((), ())), preferred_element_type=jnp.float32
        )
        finish_grads = finish_pull(grad_normed_out)
        state_grad = pass_back(scanned[2], finish_grads[4])
        decay_grad = jnp.sum(state_grad * incoming, axis=(1, 2))
        scan_grads = scan_pull(
            (
                finish_grads[0],
                state_grad,
                decay_grad,
                finish_grads[1],
                finish_grads[2],
                finish_grads[3],
            )
        )
        conv_grad = scan_grads[0].astype(jnp.bfloat16).astype(jnp.float32)
        extended_wide = extended.astype(jnp.float32)
        taps_wide = gathered[2].astype(jnp.float32)
        grad_conv_weight = jnp.stack(
            [
                jnp.sum(conv_grad * extended_wide[tap_idx : tap_idx + length], axis=0)
                for tap_idx in range(rim_rows + 1)
            ]
        )
        grad_conv_bias = jnp.sum(conv_grad, axis=0)
        grad_extended = jnp.zeros((length + rim_rows, conv_grad.shape[1]), jnp.float32)
        for tap_idx in range(rim_rows + 1):
            grad_extended = grad_extended + jnp.pad(
                taps_wide[tap_idx] * conv_grad, ((tap_idx, rim_rows - tap_idx), (0, 0))
            )
        returned = passed_along(grad_extended[:rim_rows], "seq", -1)
        grad_conv_in = grad_extended[rim_rows:] + jnp.pad(
            returned, ((length - rim_rows, 0), (0, 0))
        )
        grad_projected = jnp.concatenate(
            [finish_grads[5], grad_conv_in, scan_grads[1]], axis=1
        ).astype(jnp.bfloat16)
        grad_in_weight = lax.dot_general(
            normed_low, grad_projected, (((0,), (0,)), ((), ())), preferred_element_type=jnp.float32
        )
        grad_normed = lax.dot_general(
            grad_projected,
            gathered[1],
            (((1,), (1,)), ((), ())),
            preferred_element_type=jnp.float32,
        )
        norm_value, norm_pull = jax.vjp(rms_norm, hidden_in, gathered[0].astype(jnp.float32))
        grad_input_part, grad_norm_gain = norm_pull(grad_normed)
        grad_hidden = grad_hidden + grad_input_part
        owned = (
            lax.psum_scatter(
                grad_norm_gain.astype(jnp.bfloat16), "dp", scatter_dimension=0, tiled=True
            ).astype(jnp.float32),
            lax.psum_scatter(
                grad_in_weight.astype(jnp.bfloat16), "dp", scatter_dimension=0, tiled=True
            ).astype(jnp.float32),
            lax.psum_scatter(
                grad_conv_weight.astype(jnp.bfloat16), "dp", scatter_dimension=1, tiled=True
            ).astype(jnp.float32),
            lax.psum_scatter(
                grad_conv_bias.astype(jnp.bfloat16), "dp", scatter_dimension=0, tiled=True
            ).astype(jnp.float32),
            lax.psum_scatter(
                scan_grads[2].astype(jnp.bfloat16), "dp", scatter_dimension=0, tiled=True
            ).astype(jnp.float32),
            lax.psum_scatter(
                scan_grads[3].astype(jnp.bfloat16), "dp", scatter_dimension=0, tiled=True
            ).astype(jnp.float32),
            lax.psum_scatter(
                finish_grads[6].astype(jnp.bfloat16), "dp", scatter_dimension=0, tiled=True
            ).astype(jnp.float32),
            lax.psum_scatter(
                finish_grads[7].astype(jnp.bfloat16), "dp", scatter_dimension=0, tiled=True
            ).astype(jnp.float32),
            lax.psum_scatter(
                grad_out_weight.astype(jnp.bfloat16), "dp", scatter_dimension=0, tiled=True
            ).astype(jnp.float32),
        )
        reduced[layer_idx] = (
            lax.psum(owned[0].astype(jnp.bfloat16), "seq").astype(jnp.float32),
            lax.psum(owned[1].astype(jnp.bfloat16), "seq").astype(jnp.float32),
            lax.psum(owned[2].astype(jnp.bfloat16), "seq").astype(jnp.float32),
            lax.psum(owned[3].astype(jnp.bfloat16), "seq").astype(jnp.float32),
            lax.psum(owned[4].astype(jnp.bfloat16), "seq").astype(jnp.float32),
            lax.psum(owned[5].astype(jnp.bfloat16), "seq").astype(jnp.float32),
            lax.psum(owned[6].astype(jnp.bfloat16), "seq").astype(jnp.float32),
            lax.psum(owned[7].astype(jnp.bfloat16), "seq").astype(jnp.float32),
            lax.psum(owned[8].astype(jnp.bfloat16), "seq").astype(jnp.float32),
        )
    stacked = tuple(
        (
            jnp.stack([reduced[layer_pos][member_idx] for layer_pos in range(layers)])
            for member_idx in range(9)
        )
    )
    return (
        hidden[None],
        grad_hidden[None],
        stacked[0],
        stacked[1],
        stacked[2],
        stacked[3],
        stacked[4],
        stacked[5],
        stacked[6],
        stacked[7],
        stacked[8],
    )


def solution(mesh):
    in_specs = (
        P("dp", "seq", None),
        P(None, "dp"),
        P(None, "dp", None),
        P(None, None, "dp"),
        P(None, "dp"),
        P(None, "dp"),
        P(None, "dp"),
        P(None, "dp"),
        P(None, "dp"),
        P(None, "dp", None),
        P("dp", "seq", None),
    )
    out_specs = (
        P("dp", "seq", None),
        P("dp", "seq", None),
        P(None, "dp"),
        P(None, "dp", None),
        P(None, None, "dp"),
        P(None, "dp"),
        P(None, "dp"),
        P(None, "dp"),
        P(None, "dp"),
        P(None, "dp"),
        P(None, "dp", None),
    )
    return jax.shard_map(body, mesh=mesh, in_specs=in_specs, out_specs=out_specs, check_vma=False)
```

profile of v0, /device:TPU:0, one launch (start us, length us, event | category | flops | bytes accessed | tf_op | source)
XLA Modules:
  0.0 1561.0 jit_solution(4818492437121443133)
XLA Ops:
  27.3 25.1 %all-gather.1 = bf16[1,4,2304]{1,0,2:T(2,128)(2,1)S(1)} all-gather(bf16[1,4,576]{1,0,2:T(2,128)(2,1)S(1)} %copy.702), channel_id=3, replica_groups=mesh['dp'=4,'seq'=8] {'dp'}, dimensions={2}, use_global_device_ids=true | all-gather | bytes 23040 | tf_op jit(solution)/shard_map/all_gather | solution.py:139
  53.6 47.9 %slice_reduce_fusion.7 = (f32[2304]{0:T(1024)S(1)}, f32[2304]{0:T(1024)S(1)}, f32[2304]{0:T(1024)S(1)}, f32[2304]{0:T(1024)S(1)}) fusion(f32[1,4,2304]{1,0,2:T(1,128)S(1)} %convert_element_type.302), kind=kLoop, calls=%fused_computation.285 | loop fusion | bytes 73728 | tf_op jit(solution)/shard_map/slice | solution.py:31
  105.3 15.5 all-reduce.57
  138.0 16.2 %all-gather.10 = bf16[1,4,2304]{1,0,2:T(2,128)(2,1)S(1)} all-gather(bf16[1,4,576]{1,0,2:T(2,128)(2,1)S(1)} %copy.703), channel_id=12, replica_groups=mesh['dp'=4,'seq'=8] {'dp'}, dimensions={2}, use_global_device_ids=true | all-gather | bytes 23040 | tf_op jit(solution)/shard_map/all_gather | solution.py:139
  155.5 47.8 %slice_reduce_fusion.3 = (f32[2304]{0:T(1024)S(1)}, f32[2304]{0:T(1024)S(1)}, f32[2304]{0:T(1024)S(1)}, f32[2304]{0:T(1024)S(1)}) fusion(f32[1,4,2304]{1,0,2:T(1,128)S(1)} %convert_element_type.309), kind=kLoop, calls=%fused_computation.281 | loop fusion | bytes 73728 | tf_op jit(solution)/shard_map/slice | solution.py:31
  213.7 13.4 fusion.301
  270.1 19.2 %bitcast_add_fusion.5 = f32[2,256,32,64]{1,3,2,0:T(8,128)S(1)} fusion(f32[2,256,32,64]{1,3,2,0:T(8,128)S(1)} %fusion.126, f32[2,256,32]{1,2,0:T(8,128)S(1)} %get-tuple-element.301, f32[2,256,256]{2,1,0:T(8,128)S(1)} %fusion.307, f32[2,32,256]{2,1,0:T(8,128)S(1)} %get-tuple-element.299, pred[256,256]{1,0:T(8,128)(4,1)S(1)} %iota_compare_fusion, ...), kind=kOutput, calls=%fused_computation.138 | convolution fusion | flops 3236954112 | bytes 13369344 | tf_op jit(solution)/shard_map/khij,kjhp->kihp/dot_general | solution.py:54
  295.5 103.0 %while.42 = (s32[]{:T(128)}, f32[32,64,128]{2,1,0:T(8,128)S(1)}, f32[32]{0:T(128)S(1)}, f32[32,64,128]{2,1,0:T(8,128)S(1)}, s32[]{:T(128)}) while((s32[]{:T(128)}, f32[32,64,128]{2,1,0:T(8,128)S(1)}, f32[32]{0:T(128)S(1)}, f32[32,64,128]{2,1,0:T(8,128)S(1)}, s32[]{:T(128)}) %tuple.164), condition=%wide.region_6.7_spmd, body=%wide.region_5.6_spmd.sunk | while | flops 524290 | bytes 7340261 | solution.py:93
  302.3 12.5 collective-permute-start
  317.1 13.9 collective-permute-start
  333.4 13.9 collective-permute-start
  349.7 13.9 collective-permute-start
  366.0 13.9 collective-permute-start
  382.3 13.9 collective-permute-start
  420.2 11.3 fusion.302
  442.1 13.8 collective-permute-start.5
  491.8 19.3 %bitcast_add_fusion.3 = f32[2,256,32,64]{1,3,2,0:T(8,128)S(1)} fusion(f32[2,256,32,64]{1,3,2,0:T(8,128)S(1)} %fusion.123, f32[2,256,32]{1,2,0:T(8,128)S(1)} %copy-done.112, f32[2,256,256]{2,1,0:T(8,128)S(1)} %copy-done.127, f32[2,32,256]{2,1,0:T(8,128)S(1)} %copy-done.159, pred[256,256]{1,0:T(8,128)(4,1)S(1)} %copy-done.165, ...), kind=kOutput, calls=%fused_computation.132 | convolution fusion | flops 3236954112 | bytes 13369344 | tf_op jit(solution)/shard_map/khij,kjhp->kihp/dot_general | solution.py:54
  517.3 102.3 %while.43 = (s32[]{:T(128)}, f32[32,64,128]{2,1,0:T(8,128)S(1)}, f32[32]{0:T(128)S(1)}, f32[32,64,128]{2,1,0:T(8,128)S(1)}, s32[]{:T(128)}) while((s32[]{:T(128)}, f32[32,64,128]{2,1,0:T(8,128)S(1)}, f32[32]{0:T(128)S(1)}, f32[32,64,128]{2,1,0:T(8,128)S(1)}, s32[]{:T(128)}) %tuple.167), condition=%wide.region_14.15_spmd, body=%wide.region_13.14_spmd.sunk | while | flops 524290 | bytes 7340261 | solution.py:93
  524.3 11.4 collective-permute-start.1
  538.1 13.9 collective-permute-start.1
  554.4 13.9 collective-permute-start.1
  570.7 13.9 collective-permute-start.1
  587.0 13.9 collective-permute-start.1
  603.3 13.9 collective-permute-start.1
  661.8 25.8 %fusion.15 = (f32[2,32,256]{2,1,0:T(8,128)}, f32[2,32,256]{2,1,0:T(8,128)}, f32[2,256,256]{2,1,0:T(8,128)}) fusion(f32[2,256,256]{2,1,0:T(8,128)S(1)} %copy-done.128, f32[2,32,256]{2,1,0:T(8,128)S(1)} %copy-done.160, pred[256,256]{1,0:T(8,128)(4,1)S(1)} %copy-done.166, f32[2,256,32,64]{1,0,3,2:T(2,128)} %reshape.594, f32[2,256,32]{1,2,0:T(8,128)S(1)} %bitcast.645, ...), kind=kOutput, calls=%fused_computation.37 | convolution fusion | flops 3259858944 | bytes 9764864 | tf_op jit(solution)/shard_map/transpose(jvp(khij,kjhp->kihp))/dot_general | solution.py:54
  687.6 96.7 %while.44 = (s32[]{:T(128)}, f32[32,64,128]{2,1,0:T(8,128)S(1)}, f32[32]{0:T(128)S(1)}, f32[32,64,128]{2,1,0:T(8,128)S(1)}, s32[]{:T(128)}, /*index=5*/s32[]{:T(128)}) while((s32[]{:T(128)}, f32[32,64,128]{2,1,0:T(8,128)S(1)}, f32[32]{0:T(128)S(1)}, f32[32,64,128]{2,1,0:T(8,128)S(1)}, s32[]{:T(128)}, ...), condition=%wide.region_24.26_spmd.clone, body=%wide.region_23.25_spmd.clone.sunk | while | flops 1310723 | bytes 6291703 | solution.py:103
  689.9 14.3 collective-permute-done.2
  707.6 10.3 collective-permute-done.2
  813.6 19.3 %multiply_reduce_fusion.11 = (f32[2,256,32]{1,2,0:T(8,128)S(1)}, f32[2,256,32]{1,2,0:T(8,128)S(1)}, f32[2,256,32,64]{1,3,2,0:T(8,128)}) fusion(f32[2,256,32,64]{1,3,2,0:T(8,128)} %fusion.175, f32[2,256,32,64]{1,0,3,2:T(2,128)} %reshape.594, f32[2,256,32]{1,2,0:T(8,128)S(1)} %bitcast.647, f32[2,256,32,64]{1,0,3,2:T(2,128)} %reshape.611, ...), kind=kOutput, calls=%fused_computation.153 | convolution fusion | flops 3244261376 | bytes 17694848 | tf_op jit(solution)/shard_map/transpose(jvp(khij,kjhp->kihp))/dot_general | solution.py:54
  902.4 11.2 pad_add_fusion.1
  919.8 10.3 multiply_reduce_fusion.18
  952.2 14.0 convolution_convert_fusion
  966.9 12.8 multiply_reduce_fusion.5
  991.4 78.5 %while.45 = (s32[]{:T(128)}, f32[32,64,128]{2,1,0:T(8,128)S(1)}, f32[32]{0:T(128)S(1)}, f32[32,64,128]{2,1,0:T(8,128)S(1)}, s32[]{:T(128)}, /*index=5*/s32[]{:T(128)}) while((s32[]{:T(128)}, f32[32,64,128]{2,1,0:T(8,128)S(1)}, f32[32]{0:T(128)S(1)}, f32[32,64,128]{2,1,0:T(8,128)S(1)}, s32[]{:T(128)}, ...), condition=%wide.region_48.50_spmd.clone, body=%wide.region_47.49_spmd.clone.sunk | while | flops 1310723 | bytes 6291703 | solution.py:103
  992.9 9.8 collective-permute-done.3
  1004.4 9.6 collective-permute-done.3
  1015.6 9.6 collective-permute-done.3
  1078.7 16.7 %multiply_reduce_fusion.6 = (f32[2,256,32]{1,2,0:T(8,128)S(1)}, f32[2,256,32]{1,2,0:T(8,128)S(1)}, f32[2,256,32,64]{1,3,2,0:T(8,128)}) fusion(f32[2,256,32,64]{1,3,2,0:T(8,128)S(1)} %fusion.176, f32[2,256,32,64]{1,0,3,2:T(2,128)S(1)} %copy-done.21, f32[2,256,32]{1,2,0:T(8,128)S(1)} %bitcast.640, f32[2,256,32,64]{1,0,3,2:T(2,128)S(1)} %copy-done, ...), kind=kOutput, calls=%fused_computation.143 | convolution fusion | flops 3244261376 | bytes 17694848 | tf_op jit(solution)/shard_map/transpose(jvp(khij,kjhp->kihp))/dot_general | solution.py:54
  1109.0 24.4 %fusion.17 = (f32[2,32,256]{2,1,0:T(8,128)S(1)}, f32[2,32,256]{2,1,0:T(8,128)S(1)}, f32[2,256,256]{2,1,0:T(8,128)}) fusion(f32[2,256,256]{2,1,0:T(8,128)} %copy-done.125, f32[2,32,256]{2,1,0:T(8,128)S(1)} %copy-done.158, pred[256,256]{1,0:T(8,128)(4,1)} %copy-done.164, f32[2,256,32,64]{1,0,3,2:T(2,128)S(1)} %copy-done.22, f32[2,256,32]{1,2,0:T(8,128)S(1)} %bitcast.641, ...), kind=kOutput, calls=%fused_computation.39 | convolution fusion | flops 3259858944 | bytes 9764864 | tf_op jit(solution)/shard_map/transpose(jvp(khij,kjhp->kihp))/dot_general | solution.py:54
  1186.2 14.7 fusion.56
  1211.5 10.4 pad_add_fusion
  1229.0 13.4 convolution_convert_fusion.1
  1259.1 83.6 %reduce-scatter.11.cloned.1.call-done = bf16[256,4384]{0,1:T(8,128)(2,1)} async-done(((bf16[1024,4384]{0,1:T(8,128)(2,1)}), bf16[256,4384]{0,1:T(8,128)(2,1)}) %reduce-scatter.11.cloned.1.call-update) | async-done | bytes 2244624 | tf_op jit(solution)/shard_map/reduce_scatter | solution.py:274
  1342.8 28.0 %reduce-scatter.21.cloned.1.call-done = bf16[576,4]{1,0:T(8,128)(2,1)} async-done(((bf16[2304,4]{1,0:T(8,128)(2,1)}), bf16[576,4]{1,0:T(8,128)(2,1)}) %reduce-scatter.21.cloned.1.call-update) | async-done | bytes 4624
  1371.8 11.2 multiply_reduce_fusion.19
  1383.0 15.4 all-reduce.56
  1404.3 27.4 %all-reduce.54 = (bf16[1,256]{1,0:T(2,128)(2,1)S(1)}, bf16[1,256]{1,0:T(2,128)(2,1)S(1)}, bf16[1,4,576]{2,1,0:T(4,128)(2,1)S(1)}, bf16[1,4,576]{2,1,0:T(4,128)(2...) all-reduce(bf16[1,256]{1,0:T(2,128)(2,1)S(1)} %stack.187, ...), channel_id=1, replica_groups=mesh['dp'=4,'seq'=8] {'seq'}, use_global_device_ids=true, to_apply=%region_69.71 | all-reduce | flops 7344 | bytes 29376 | tf_op jit(solution)/shard_map/psum | solution.py:300
  1435.8 109.5 %all-reduce.60.cloned.1.call-done = (bf16[1,256,4384]{1,2,0:T(8,128)(2,1)}, bf16[1,256,4384]{1,2,0:T(8,128)(2,1)}, bf16[1,512,1024]{2,1,0:T(8,128)(2,1)}, bf16[1,512,1024]{2,1,0:T(8,128)(2,1)}) async-done(((bf16[1,256,4384]{1,2,0:T(8,128)(2,1)}, bf16[1,256,4384]{1,2,0:T(8,128)(2,1)}, bf16[1,512,1024]{2,1,0:T(8,128)(2,1)}, bf16[1,512,1024]{2,1,0:T(8,128)(2,1)}), (bf16[1,256,4384]{1,2,0:T(8,128)(2,1)}, ...) | async-done | bytes 6586384 | tf_op jit(solution)/shard_map/psum | solution.py:301
  (898 shorter events, 643.9 us)
Async XLA Ops:
  7.2 206.5 %all-gather.23.cloned.1.call-start = ((), (), s32[]{:S(2)}) async-start(), calls=%async_computation.10 | async-start | bytes 11223040 | tf_op jit(solution)/shard_map/all_gather | solution.py:138
  12.0 400.8 %all-gather.25.cloned.1.call-start = ((), (), s32[]{:S(2)}) async-start(), calls=%async_computation.11 | async-start | bytes 5242880 | tf_op jit(solution)/shard_map/all_gather | solution.py:145
  15.2 404.9 %all-gather.27.cloned.1.call-start = ((), (), s32[]{:S(2)}) async-start(), calls=%async_computation.12 | async-start | bytes 11223040 | tf_op jit(solution)/shard_map/all_gather | solution.py:138
  16.0 618.5 %all-gather.29.cloned.1.call-start = ((), (), s32[]{:S(2)}) async-start(), calls=%async_computation.13 | async-start | bytes 5242880 | tf_op jit(solution)/shard_map/all_gather | solution.py:145
  16.5 1242.5 %reduce-scatter.17.cloned.1.call-start = ((), (), s32[]{:S(2)}) async-start(), calls=%async_computation.9 | async-start | bytes 5242880 | tf_op jit(solution)/shard_map/reduce_scatter | solution.py:295
  16.6 252.1 %copy-start.164 = (pred[256,256]{1,0:T(8,128)(4,1)}, pred[256,256]{1,0:T(8,128)(4,1)S(1)}, u32[]{:S(2)}) copy-start(pred[256,256]{1,0:T(8,128)(4,1)S(1)} %iota_compare_fusion) | copy-start | bytes 196612
  129.1 283.7 %copy-start.190 = (f32[1,2048]{1,0:T(1,128)}, f32[1,2048]{1,0:T(1,128)S(1)}, u32[]{:S(2)}) copy-start(f32[1,2048]{1,0:T(1,128)S(1)} %convert_element_type.307) | copy-start | bytes 24580
  203.3 256.9 %copy-start.150 = (f32[2304]{0:T(1024)}, f32[2304]{0:T(1024)S(1)}, u32[]{:S(2)}) copy-start(f32[2304]{0:T(1024)S(1)} %get-tuple-element.168) | copy-start | bytes 27652
  203.3 256.9 %copy-start.152 = (f32[2304]{0:T(1024)}, f32[2304]{0:T(1024)S(1)}, u32[]{:S(2)}) copy-start(f32[2304]{0:T(1024)S(1)} %get-tuple-element.169) | copy-start | bytes 27652
  203.3 256.9 %copy-start.154 = (f32[2304]{0:T(1024)}, f32[2304]{0:T(1024)S(1)}, u32[]{:S(2)}) copy-start(f32[2304]{0:T(1024)S(1)} %get-tuple-element.170) | copy-start | bytes 27652
  236.0 3.4 collective-permute-start.4
  295.7 6.4 collective-permute-start
  302.3 14.7 collective-permute-start
  317.1 16.1 %collective-permute-start = (f32[32,64,128]{2,1,0:T(8,128)S(1)}, f32[32,64,128]{2,1,0:T(8,128)S(1)}, u32[]{:S(2)}, u32[]{:S(2)}) collective-permute-start(f32[32,64,128]{2,1,0:T(8,128)S(1)} %multiply_add_fusion.16), channel_id=1, source_target_pairs={{0,1},{1,2},{2,3},{3,4},{4,5},{5,6},{6,7},{8,9},{9,10},{10,11},{11... | collective-permute-start | bytes 3145736 | tf_op jit(solution)/shard_map/while/body/eval_jaxpr/ppermute | solution.py:21
  333.4 16.1 %collective-permute-start = (f32[32,64,128]{2,1,0:T(8,128)S(1)}, f32[32,64,128]{2,1,0:T(8,128)S(1)}, u32[]{:S(2)}, u32[]{:S(2)}) collective-permute-start(f32[32,64,128]{2,1,0:T(8,128)S(1)} %multiply_add_fusion.16), channel_id=1, source_target_pairs={{0,1},{1,2},{2,3},{3,4},{4,5},{5,6},{6,7},{8,9},{9,10},{10,11},{11... | collective-permute-start | bytes 3145736 | tf_op jit(solution)/shard_map/while/body/eval_jaxpr/ppermute | solution.py:21
  349.7 16.1 %collective-permute-start = (f32[32,64,128]{2,1,0:T(8,128)S(1)}, f32[32,64,128]{2,1,0:T(8,128)S(1)}, u32[]{:S(2)}, u32[]{:S(2)}) collective-permute-start(f32[32,64,128]{2,1,0:T(8,128)S(1)} %multiply_add_fusion.16), channel_id=1, source_target_pairs={{0,1},{1,2},{2,3},{3,4},{4,5},{5,6},{6,7},{8,9},{9,10},{10,11},{11... | collective-permute-start | bytes 3145736 | tf_op jit(solution)/shard_map/while/body/eval_jaxpr/ppermute | solution.py:21
  366.0 16.1 %collective-permute-start = (f32[32,64,128]{2,1,0:T(8,128)S(1)}, f32[32,64,128]{2,1,0:T(8,128)S(1)}, u32[]{:S(2)}, u32[]{:S(2)}) collective-permute-start(f32[32,64,128]{2,1,0:T(8,128)S(1)} %multiply_add_fusion.16), channel_id=1, source_target_pairs={{0,1},{1,2},{2,3},{3,4},{4,5},{5,6},{6,7},{8,9},{9,10},{10,11},{11... | collective-permute-start | bytes 3145736 | tf_op jit(solution)/shard_map/while/body/eval_jaxpr/ppermute | solution.py:21
  382.3 16.1 %collective-permute-start = (f32[32,64,128]{2,1,0:T(8,128)S(1)}, f32[32,64,128]{2,1,0:T(8,128)S(1)}, u32[]{:S(2)}, u32[]{:S(2)}) collective-permute-start(f32[32,64,128]{2,1,0:T(8,128)S(1)} %multiply_add_fusion.16), channel_id=1, source_target_pairs={{0,1},{1,2},{2,3},{3,4},{4,5},{5,6},{6,7},{8,9},{9,10},{10,11},{11... | collective-permute-start | bytes 3145736 | tf_op jit(solution)/shard_map/while/body/eval_jaxpr/ppermute | solution.py:21
  442.1 17.8 %collective-permute-start.5 = (bf16[3,2304]{1,0:T(4,128)(2,1)S(1)}, bf16[3,2304]{1,0:T(4,128)(2,1)S(1)}, u32[]{:S(2)}, u32[]{:S(2)}) collective-permute-start(bf16[3,2304]{1,0:T(4,128)(2,1)S(1)} %copy.547), channel_id=1, source_target_pairs={{0,1},{1,2},{2,3},{3,4},{4,5},{5,6},{6,7},{8,9},{9,10},{10,11},{11... | collective-permute-start | bytes 41480 | tf_op jit(solution)/shard_map/ppermute | solution.py:21
  517.5 6.7 collective-permute-start.1
  524.3 13.7 collective-permute-start.1
  538.1 16.1 %collective-permute-start.1 = (f32[32,64,128]{2,1,0:T(8,128)S(1)}, f32[32,64,128]{2,1,0:T(8,128)S(1)}, u32[]{:S(2)}, u32[]{:S(2)}) collective-permute-start(f32[32,64,128]{2,1,0:T(8,128)S(1)} %multiply_add_fusion.17), channel_id=1, source_target_pairs={{0,1},{1,2},{2,3},{3,4},{4,5},{5,6},{6,7},{8,9},{9,10},{10,11},{11... | collective-permute-start | bytes 3145736 | tf_op jit(solution)/shard_map/while/body/eval_jaxpr/ppermute | solution.py:21
  554.4 16.1 %collective-permute-start.1 = (f32[32,64,128]{2,1,0:T(8,128)S(1)}, f32[32,64,128]{2,1,0:T(8,128)S(1)}, u32[]{:S(2)}, u32[]{:S(2)}) collective-permute-start(f32[32,64,128]{2,1,0:T(8,128)S(1)} %multiply_add_fusion.17), channel_id=1, source_target_pairs={{0,1},{1,2},{2,3},{3,4},{4,5},{5,6},{6,7},{8,9},{9,10},{10,11},{11... | collective-permute-start | bytes 3145736 | tf_op jit(solution)/shard_map/while/body/eval_jaxpr/ppermute | solution.py:21
  570.7 16.1 %collective-permute-start.1 = (f32[32,64,128]{2,1,0:T(8,128)S(1)}, f32[32,64,128]{2,1,0:T(8,128)S(1)}, u32[]{:S(2)}, u32[]{:S(2)}) collective-permute-start(f32[32,64,128]{2,1,0:T(8,128)S(1)} %multiply_add_fusion.17), channel_id=1, source_target_pairs={{0,1},{1,2},{2,3},{3,4},{4,5},{5,6},{6,7},{8,9},{9,10},{10,11},{11... | collective-permute-start | bytes 3145736 | tf_op jit(solution)/shard_map/while/body/eval_jaxpr/ppermute | solution.py:21
  587.0 16.1 %collective-permute-start.1 = (f32[32,64,128]{2,1,0:T(8,128)S(1)}, f32[32,64,128]{2,1,0:T(8,128)S(1)}, u32[]{:S(2)}, u32[]{:S(2)}) collective-permute-start(f32[32,64,128]{2,1,0:T(8,128)S(1)} %multiply_add_fusion.17), channel_id=1, source_target_pairs={{0,1},{1,2},{2,3},{3,4},{4,5},{5,6},{6,7},{8,9},{9,10},{10,11},{11... | collective-permute-start | bytes 3145736 | tf_op jit(solution)/shard_map/while/body/eval_jaxpr/ppermute | solution.py:21
  603.3 16.1 %collective-permute-start.1 = (f32[32,64,128]{2,1,0:T(8,128)S(1)}, f32[32,64,128]{2,1,0:T(8,128)S(1)}, u32[]{:S(2)}, u32[]{:S(2)}) collective-permute-start(f32[32,64,128]{2,1,0:T(8,128)S(1)} %multiply_add_fusion.17), channel_id=1, source_target_pairs={{0,1},{1,2},{2,3},{3,4},{4,5},{5,6},{6,7},{8,9},{9,10},{10,11},{11... | collective-permute-start | bytes 3145736 | tf_op jit(solution)/shard_map/while/body/eval_jaxpr/ppermute | solution.py:21
  688.6 15.6 collective-permute-start.2
  706.4 11.5 collective-permute-start.2
  720.1 10.8 collective-permute-start.2
  733.1 10.8 collective-permute-start.2
  746.1 10.8 collective-permute-start.2
  759.0 10.8 collective-permute-start.2
  772.0 10.8 collective-permute-start.2
  859.5 399.6 %reduce-scatter.15.cloned.1.call-start = ((), (), s32[]{:S(2)}) async-start(), calls=%async_computation.8 | async-start | bytes 5242880 | tf_op jit(solution)/shard_map/reduce_scatter | solution.py:295
  900.9 14.3 collective-permute-start.6
  937.3 321.8 %reduce-scatter.13.cloned.1.call-start = ((), (), s32[]{:S(2)}) async-start(), calls=%async_computation.7 | async-start | bytes 11223040 | tf_op jit(solution)/shard_map/reduce_scatter | solution.py:274
  966.2 376.5 %reduce-scatter.11.cloned.1.call-start = ((), (), s32[]{:S(2)}) async-start(), calls=%async_computation.6 | async-start | bytes 11223040 | tf_op jit(solution)/shard_map/reduce_scatter | solution.py:274
  991.6 11.1 collective-permute-start.3
  1003.1 10.9 collective-permute-start.3
  1014.3 10.9 collective-permute-start.3
  1025.5 10.9 collective-permute-start.3
  1036.8 10.9 collective-permute-start.3
  1048.0 10.9 collective-permute-start.3
  1059.2 10.5 collective-permute-start.3
  1210.1 12.9 collective-permute-start.7
  1242.4 128.3 %reduce-scatter.21.cloned.1.call-start = ((), (), s32[]{:S(2)}) async-start(), calls=%async_computation.15 | async-start | bytes 737280
  1246.4 156.9 %reduce-scatter.19.cloned.1.call-start = ((), (), s32[]{:S(2)}) async-start(), calls=%async_computation.14 | async-start | bytes 737280
  1255.9 289.4 %all-reduce.60.cloned.1.call-start = ((), (), s32[]{:S(2)}) async-start(), calls=%async_computation.16 | async-start | bytes 13172736 | tf_op jit(solution)/shard_map/psum | solution.py:301
  (240 other events, 4213.9 us)
Sparse Core Ops, SparseCore 0:
  12.1 105.0 all-gather.22
  119.6 58.8 all-gather.24
  180.3 92.4 all-gather.26
  274.5 52.7 all-gather.28
  859.6 58.5 reduce-scatter.16
  937.4 60.1 reduce-scatter.14
  1000.7 91.2 reduce-scatter.12
  1242.5 100.1 reduce-scatter.10
  1345.6 25.0 reduce-scatter.20
  1373.7 25.1 reduce-scatter.18
  1401.6 143.6 all-reduce.59
where the time goes:
time: 1570 us; the launch traced here: 1560 us
  waiting for transfers between devices  393 us (25%)
  matrix products  350 us (22%)
  local copies, waits for them, and re-layouts  234 us (15%)
  other arithmetic  220 us (14%)
  starting transfers between devices  209 us (13%)
  blocking collectives  132 us (8%)
  between operations  21.6 us (1%)
    ppermute x32, starting transfers between devices, passed_along(): lax.ppermute(value, axis, [(source, source + steps) for source in range(f...  208 us
    ppermute x32, waiting for transfers between devices, passed_along(): lax.ppermute(value, axis, [(source, source + steps) for source in range(f...  170 us
    dot_general x6, matrix products, shard_scan(): jnp.einsum('khij,kjhp->kihp', decays * scores[:, None], scaled, precision...  125 us
    psum x1, waiting for transfers between devices, body(): lax.psum(owned[1].astype(jnp.bfloat16), 'seq').astype(jnp.float32)  109 us
    slice x2, local copies, waits for them, and re-layouts, conv_apply(): conv_weight[tap_idx]  95.7 us
    reduce_scatter x2, waiting for transfers between devices, body(): lax.psum_scatter(grad_in_weight.astype(jnp.bfloat16), 'dp', scatter_dimen...  83.7 us
    unnamed x526, local copies, waits for them, and re-layouts  59.3 us
    all_gather x2, blocking collectives, body(): lax.all_gather(shards[2], 'dp', axis=1, tiled=True)  41.3 us
  transfers between devices with their start and end apart: 43, of which 31 were waited for; matrix products, arithmetic and copies ran while one was open for 39% of the time, Pallas kernels for 0%

commit v1 on v0

v1 whole, which is shorter than its diff:
```python
import functools

import jax
import jax.numpy as jnp
from jax import lax
from jax.experimental import pallas as pl
from jax.experimental.pallas import tpu as pltpu
from jax.sharding import PartitionSpec as P

HEADS = 32
HEAD_DIM = 64
STATE = 128
GROUP = 256
INNER = 2048
XBC = 2304
CHUNKS = 8


epsilon = 1e-05
highest = lax.Precision.HIGHEST
plain = lax.Precision.DEFAULT


def passed_along(value, axis, steps):
    count = lax.axis_size(axis)
    first, last = (max(0, -steps), min(count, count - steps))
    return lax.ppermute(value, axis, [(source, source + steps) for source in range(first, last)])


def rms_norm(values, gain):
    return values * lax.rsqrt(jnp.mean(values * values, axis=-1, keepdims=True) + epsilon) * gain


def chain_kernel(count, step, decay_ref, local_ref, out_ref, send, held, send_sem, recv_sem):
    me = lax.axis_index("seq")
    place = me if step > 0 else count - 1 - me
    has_source = place > 0
    has_target = place < count - 1
    barrier = pltpu.get_barrier_semaphore()

    @pl.when(has_source)
    def _():
        pl.semaphore_signal(
            barrier, inc=1, device_id={"seq": me - step}, device_id_type=pl.DeviceIdType.MESH
        )

    @pl.when(has_target)
    def _():
        pl.semaphore_wait(barrier, 1)

    width = out_ref.shape[0] // CHUNKS

    def copy_of(chunk):
        return pltpu.make_async_remote_copy(
            src_ref=send.at[chunk],
            dst_ref=held.at[chunk],
            send_sem=send_sem.at[chunk],
            recv_sem=recv_sem.at[chunk],
            device_id={"seq": me + step},
            device_id_type=pl.DeviceIdType.MESH,
        )

    for chunk in range(CHUNKS):
        part = pl.ds(chunk * width, width)

        @pl.when(has_source)
        def _():
            copy_of(chunk).wait_recv()
            out_ref[part] = held[chunk].astype(jnp.float32)

        @pl.when(jnp.logical_not(has_source))
        def _():
            out_ref[part] = jnp.zeros((width,) + out_ref.shape[1:], jnp.float32)

        @pl.when(has_target)
        def _():
            send[chunk] = (decay_ref[part] * out_ref[part] + local_ref[part]).astype(jnp.bfloat16)
            copy_of(chunk).start()

    @pl.when(has_target)
    def _():
        for chunk in range(CHUNKS):
            copy_of(chunk).wait_send()


def chain(decay, local, step):
    count = lax.axis_size("seq")
    shape = (HEADS, HEAD_DIM, STATE)
    pieces = (CHUNKS, HEADS // CHUNKS, HEAD_DIM, STATE)
    return pl.pallas_call(
        functools.partial(chain_kernel, count, step),
        out_shape=jax.ShapeDtypeStruct(shape, jnp.float32),
        in_specs=[pl.BlockSpec(memory_space=pltpu.VMEM)] * 2,
        out_specs=pl.BlockSpec(memory_space=pltpu.VMEM),
        scratch_shapes=[
            pltpu.VMEM(pieces, jnp.bfloat16),
            pltpu.VMEM(pieces, jnp.bfloat16),
            pltpu.SemaphoreType.DMA((CHUNKS,)),
            pltpu.SemaphoreType.DMA((CHUNKS,)),
        ],
        cost_estimate=pl.CostEstimate(flops=2**20, bytes_accessed=2**25, transcendentals=0),
        compiler_params=pltpu.CompilerParams(
            collective_id=0 if step > 0 else 1,
            has_side_effects=True,
            vmem_limit_bytes=16 * 2**20,
        ),
    )(jnp.broadcast_to(decay[:, None, None], (HEADS, 1, STATE)), local)


def conv_apply(extended, conv_weight, conv_bias, length):
    total = conv_bias + jnp.zeros((length, conv_bias.shape[0]), jnp.float32)
    for tap_idx in range(conv_weight.shape[0]):
        total = total + conv_weight[tap_idx] * extended[tap_idx : tap_idx + length].astype(
            jnp.float32
        )
    return total


def shard_parts(conv_out, dt_raw, dt_bias, a_log):
    length = conv_out.shape[0]
    blocks = length // GROUP
    active = jax.nn.silu(conv_out)
    values = active[:, :INNER].reshape(blocks, GROUP, HEADS, HEAD_DIM)
    b_mat = active[:, INNER : INNER + STATE].reshape(blocks, GROUP, STATE)
    c_mat = active[:, INNER + STATE :].reshape(blocks, GROUP, STATE)
    step_size = jax.nn.softplus(dt_raw + dt_bias)
    log_decay = (step_size * -jnp.exp(a_log)).reshape(blocks, GROUP, HEADS)
    causal = lax.broadcasted_iota(jnp.int32, (GROUP, GROUP), 0) >= lax.broadcasted_iota(
        jnp.int32, (GROUP, GROUP), 1
    )
    group_sum = jnp.einsum("ij,kjh->kih", causal.astype(jnp.float32), log_decay, precision=highest)
    scaled = values * step_size.reshape(blocks, GROUP, HEADS)[:, :, :, None]
    tails = jnp.exp(group_sum[:, -1:, :] - group_sum)
    group_states = jnp.einsum(
        "kjhp,kjn->khpn", scaled * tails[:, :, :, None], b_mat, precision=plain
    )
    group_decay = jnp.exp(group_sum[:, -1, :])
    return values, b_mat, c_mat, group_sum, scaled, group_states, group_decay, causal


def run_states(start, group_states, group_decay):
    entering, running = [], start
    for block_idx in range(group_states.shape[0]):
        entering.append(running)
        running = group_decay[block_idx][:, None, None] * running + group_states[block_idx]
    return jnp.stack(entering), running


def shard_scan(conv_out, dt_raw, dt_bias, a_log, skip_gain, incoming):
    length = conv_out.shape[0]
    values, b_mat, c_mat, group_sum, scaled, group_states, group_decay, causal = shard_parts(
        conv_out, dt_raw, dt_bias, a_log
    )
    by_head = jnp.swapaxes(group_sum, 1, 2)
    decays = jnp.exp(jnp.where(causal, by_head[:, :, :, None] - by_head[:, :, None, :], -jnp.inf))
    scores = jnp.einsum("kin,kjn->kij", c_mat, b_mat, precision=plain)
    within = jnp.einsum("khij,kjhp->kihp", decays * scores[:, None], scaled, precision=plain)
    entering, final = run_states(incoming, group_states, group_decay)
    carried = jnp.einsum("kin,khpn->kihp", c_mat, entering, precision=plain)
    mixed = (
        within + jnp.exp(group_sum)[:, :, :, None] * carried + skip_gain[:, None] * values
    )
    return mixed.reshape(length, INNER), final


def finish(mixed, gate_z, gate_gain):
    return rms_norm(mixed * jax.nn.silu(gate_z), gate_gain)


SMALL = (0, 2, 3, 4, 5, 6, 7)


def body(
    inputs,
    norm_gain,
    in_weight,
    conv_weight,
    conv_bias,
    dt_bias,
    a_log,
    skip_gain,
    gate_gain,
    out_weight,
    cotangent,
):
    layers = in_weight.shape[0]
    hidden = inputs[0]
    length = hidden.shape[0]
    taps = conv_weight.shape[1]
    rim_rows = taps - 1
    owners = lax.axis_size("dp")

    small = (norm_gain, conv_weight, conv_bias, dt_bias, a_log, skip_gain, gate_gain)
    extents = [member.reshape(layers, -1).shape[1] for member in small]
    starts = [sum(extents[:idx]) for idx in range(len(extents) + 1)]
    packed = jnp.concatenate([member.reshape(layers, -1) for member in small], axis=1)
    packed = lax.all_gather(packed.reshape(-1), "dp").astype(jnp.float32)
    packed = packed.reshape(owners, layers, -1)

    def small_of(layer_idx, member_idx):
        own = packed[:, layer_idx, starts[member_idx] : starts[member_idx + 1]]
        if member_idx != 1:
            return own.reshape(-1)
        return jnp.swapaxes(own.reshape(owners, taps, -1), 0, 1).reshape(taps, -1)

    def gather(shard):
        return lax.all_gather(shard, "dp", axis=0, tiled=True)

    saved = []
    for layer_idx in range(layers):
        gains = [small_of(layer_idx, member_idx) for member_idx in range(len(small))]
        conv_proj = gather(in_weight[layer_idx][:, INNER:])
        gate_proj = gather(in_weight[layer_idx][:, :INNER])
        out_proj = gather(out_weight[layer_idx])
        normed_low = rms_norm(hidden, gains[0]).astype(jnp.bfloat16)
        projected = jnp.dot(normed_low, conv_proj, preferred_element_type=jnp.float32)
        conv_in = projected[:, :XBC].astype(jnp.bfloat16)
        dt_raw = projected[:, XBC:]
        arrived = passed_along(conv_in[length - rim_rows :], "seq", 1)
        extended = jnp.concatenate([arrived, conv_in], axis=0)
        conv_out = conv_apply(extended, gains[1], gains[2], length)
        parts = shard_parts(conv_out, dt_raw, gains[3], gains[4])
        group_states, group_decay = parts[5], parts[6]
        local_state = run_states(
            jnp.zeros((HEADS, HEAD_DIM, STATE), jnp.float32), group_states, group_decay
        )[1]
        shard_decay = jnp.prod(group_decay, axis=0)
        incoming = chain(shard_decay, local_state, 1)
        gate_z = jnp.dot(normed_low, gate_proj, preferred_element_type=jnp.float32)
        (mixed, _), scan_pull = jax.vjp(
            lambda *args: shard_scan(*args, incoming),
            conv_out,
            dt_raw,
            gains[3],
            gains[4],
            gains[5],
        )
        normed_out, finish_pull = jax.vjp(finish, mixed, gate_z, gains[6])
        low_out = normed_out.astype(jnp.bfloat16)
        branch = jnp.dot(low_out, out_proj, preferred_element_type=jnp.float32)
        saved.append(
            (
                hidden,
                normed_low,
                extended,
                parts[2],
                parts[3],
                group_decay,
                shard_decay,
                low_out,
                scan_pull,
                finish_pull,
                gains,
                (conv_proj, gate_proj, out_proj),
            )
        )
        hidden = hidden + branch

    last_sum = [None]

    def summed(grad):
        part = lax.psum_scatter(
            grad.astype(jnp.bfloat16), "dp", scatter_dimension=0, tiled=True
        )
        if last_sum[0] is not None:
            part, _ = lax.optimization_barrier((part, last_sum[0]))
        last_sum[0] = lax.psum(part, "seq")
        return last_sum[0]

    def outer(left, right):
        return lax.dot_general(
            left, right, (((0,), (0,)), ((), ())), preferred_element_type=jnp.float32
        )

    def times_transposed(left, right):
        return lax.dot_general(
            left, right, (((1,), (1,)), ((), ())), preferred_element_type=jnp.float32
        )

    grad_hidden = cotangent[0]
    grad_in, grad_out, grad_small = [None] * layers, [None] * layers, [None] * layers
    for layer_idx in reversed(range(layers)):
        (
            hidden_in,
            normed_low,
            extended,
            c_mat,
            group_sum,
            group_decay,
            shard_decay,
            low_out,
            scan_pull,
            finish_pull,
            gains,
            (conv_proj, gate_proj, out_proj),
        ) = saved[layer_idx]
        blocks = length // GROUP
        grad_branch = grad_hidden.astype(jnp.bfloat16)
        grad_out[layer_idx] = summed(outer(low_out, grad_branch))
        grad_mixed, grad_gate_z, grad_gate_gain = finish_pull(
            times_transposed(grad_branch, out_proj)
        )
        by_block = grad_mixed.reshape(blocks, GROUP, HEADS, HEAD_DIM)
        entering_grads = jnp.einsum(
            "kihp,kin->khpn",
            jnp.exp(group_sum)[:, :, :, None] * by_block,
            c_mat,
            precision=plain,
        )
        direct = jnp.zeros_like(entering_grads[0])
        for block_idx in reversed(range(blocks)):
            direct = group_decay[block_idx][:, None, None] * direct + entering_grads[block_idx]
        state_grad = chain(shard_decay, direct, -1)
        gate_low = grad_gate_z.astype(jnp.bfloat16)
        grad_in_gate = summed(outer(normed_low, gate_low))
        grad_conv_out, grad_dt_raw, grad_dt_bias, grad_a_log, grad_skip = scan_pull(
            (grad_mixed, state_grad)
        )
        conv_grad = grad_conv_out.astype(jnp.bfloat16).astype(jnp.float32)
        extended_wide = extended.astype(jnp.float32)
        grad_conv_weight = jnp.stack(
            [
                jnp.sum(conv_grad * extended_wide[tap_idx : tap_idx + length], axis=0)
                for tap_idx in range(taps)
            ]
        )
        grad_conv_bias = jnp.sum(conv_grad, axis=0)
        grad_extended = jnp.zeros((length + rim_rows, conv_grad.shape[1]), jnp.float32)
        for tap_idx in range(taps):
            grad_extended = grad_extended + jnp.pad(
                gains[1][tap_idx] * conv_grad, ((tap_idx, rim_rows - tap_idx), (0, 0))
            )
        returned = passed_along(grad_extended[:rim_rows], "seq", -1)
        grad_conv_in = grad_extended[rim_rows:] + jnp.pad(
            returned, ((length - rim_rows, 0), (0, 0))
        )
        conv_low = jnp.concatenate([grad_conv_in, grad_dt_raw], axis=1).astype(jnp.bfloat16)
        grad_in[layer_idx] = (grad_in_gate, summed(outer(normed_low, conv_low)))
        grad_normed = times_transposed(gate_low, gate_proj) + times_transposed(
            conv_low, conv_proj
        )
        _, norm_pull = jax.vjp(rms_norm, hidden_in, gains[0])
        grad_input_part, grad_norm_gain = norm_pull(grad_normed)
        grad_hidden = grad_hidden + grad_input_part
        by_owner = [
            grad.reshape(owners, -1)
            for grad in (
                grad_norm_gain,
                jnp.swapaxes(grad_conv_weight.reshape(taps, owners, -1), 0, 1),
                grad_conv_bias,
                grad_dt_bias,
                grad_a_log,
                grad_skip,
                grad_gate_gain,
            )
        ]
        grad_small[layer_idx] = jnp.concatenate(by_owner, axis=1)
    totals = lax.psum(jnp.stack(grad_small, axis=1), ("dp", "seq"))
    mine = lax.dynamic_index_in_dim(totals, lax.axis_index("dp"), 0, keepdims=False)
    owned = [
        mine[:, starts[idx] : starts[idx + 1]].reshape(member.shape)
        for idx, member in enumerate(small)
    ]
    in_total = jnp.stack(
        [jnp.concatenate(pieces, axis=1).astype(jnp.float32) for pieces in grad_in]
    )
    out_total = jnp.stack([piece.astype(jnp.float32) for piece in grad_out])
    return (
        hidden[None],
        grad_hidden[None],
        owned[0],
        in_total,
        owned[1],
        owned[2],
        owned[3],
        owned[4],
        owned[5],
        owned[6],
        out_total,
    )


def solution(mesh):
    in_specs = (
        P("dp", "seq", None),
        P(None, "dp"),
        P(None, "dp", None),
        P(None, None, "dp"),
        P(None, "dp"),
        P(None, "dp"),
        P(None, "dp"),
        P(None, "dp"),
        P(None, "dp"),
        P(None, "dp", None),
        P("dp", "seq", None),
    )
    out_specs = (
        P("dp", "seq", None),
        P("dp", "seq", None),
        P(None, "dp"),
        P(None, "dp", None),
        P(None, None, "dp"),
        P(None, "dp"),
        P(None, "dp"),
        P(None, "dp"),
        P(None, "dp"),
        P(None, "dp"),
        P(None, "dp", None),
    )
    return jax.shard_map(body, mesh=mesh, in_specs=in_specs, out_specs=out_specs, check_vma=False)
```

time: 1570 us -> 1210 us (0.77)
  waiting for transfers between devices: 393 us -> 668 us
  starting transfers between devices: 209 us -> 7.79 us
  matrix products: 350 us -> 196 us
  blocking collectives: 132 us -> 11 us
  local copies, waits for them, and re-layouts: 234 us -> 132 us
  other arithmetic: 220 us -> 126 us
  Pallas kernels: 0 us -> 45.8 us
    psum x1 -> x7, waiting for transfers between devices: 109 us -> 373 us  [the longest x6 246 us: summed(): last_sum[0] = lax.psum(part, 'seq')]
    ppermute x32 -> x4, starting transfers between devices: 208 us -> 6.19 us  [passed_along(): lax.ppermute(value, axis, [(source, source + steps) for source in range(f...]
    all_gather x4 -> x6, waiting for transfers between devices: 0.04 us -> 174 us  [gather(): return lax.all_gather(shard, 'dp', axis=0, tiled=True)]
    ppermute x32 -> x4, waiting for transfers between devices: 170 us -> 0.01 us  [passed_along(): lax.ppermute(value, axis, [(source, source + steps) for source in range(f...]
    slice x2, local copies, waits for them, and re-layouts: 95.7 us -> 0.25 us  [conv_apply(): conv_weight[tap_idx]]
    dot_general x34 -> x40, matrix products: 216 us -> 140 us  [the longest x6 38.8 us: times_transposed(): lax.dot_general(left, right, (((1,), (1,)), ((), ())), preferred_element_...]
    dot_general x6, matrix products: 125 us -> 56.3 us  [shard_scan(): jnp.einsum('khij,kjhp->kihp', decays * scores[:, None], scaled, precision...]
    all_gather x6 -> x1, blocking collectives: 73.6 us -> 11 us  [body(): packed = lax.all_gather(packed.reshape(-1), 'dp').astype(jnp.float32)]
  transfers between devices with their start and end apart: 43 -> 23, of which waited for: 31 -> 15; matrix products, arithmetic and copies ran while one was open for 39% -> 34% of each run, Pallas kernels for 0% -> 4%
where the time goes in v1:
time: 1210 us
  waiting for transfers between devices  668 us (55%)
  matrix products  196 us (16%)
  local copies, waits for them, and re-layouts  132 us (11%)
  other arithmetic  126 us (10%)
  Pallas kernels  45.8 us (4%)
  between operations  17.2 us (1%)
    psum x6, waiting for transfers between devices, summed(): last_sum[0] = lax.psum(part, 'seq')  246 us
    all_gather x6, waiting for transfers between devices, gather(): return lax.all_gather(shard, 'dp', axis=0, tiled=True)  174 us
    psum x1, waiting for transfers between devices, body(): totals = lax.psum(jnp.stack(grad_small, axis=1), ('dp', 'seq'))  126 us
    reduce_scatter x6, waiting for transfers between devices, summed(): lax.psum_scatter(grad.astype(jnp.bfloat16), 'dp', scatter_dimension=0, ti...  121 us
    dot_general x6, matrix products, shard_scan(): jnp.einsum('khij,kjhp->kihp', decays * scores[:, None], scaled, precision...  56.3 us
    unnamed x423, local copies, waits for them, and re-layouts  47.5 us
    pallas_call x4, Pallas kernels, chain(): pl.pallas_call(functools.partial(chain_kernel, count, step), out_shape=ja...  45.8 us
    dot_general x6, matrix products, times_transposed(): lax.dot_general(left, right, (((1,), (1,)), ((), ())), preferred_element_...  38.8 us
  transfers between devices with their start and end apart: 23, of which 15 were waited for; matrix products, arithmetic and copies ran while one was open for 34% of the time, Pallas kernels for 4%

profile of v1, /device:TPU:0, one launch (start us, length us, event | category | flops | bytes accessed | tf_op | source)
XLA Modules:
  0.0 1205.1 jit_solution(8536235335002567618)
XLA Ops:
  22.5 11.0 all-gather.2
  40.2 33.4 %all-gather.10.cloned.1.call-done = bf16[1024,2336]{0,1:T(8,128)(2,1)} async-done(((bf16[256,2336]{0,1:T(8,128)(2,1)}), bf16[1024,2336]{0,1:T(8,128)(2,1)}) %all-gather.10.cloned.1.call-update) | async-done | bytes 4784144 | tf_op jit(solution)/shard_map/all_gather | solution.py:207
  86.4 6.8 fusion.51
  97.3 5.9 reshape.487
  114.3 5.1 fusion.73
  128.1 10.7 multiply_reduce_fusion.15
  138.8 44.4 %all-gather.18.cloned.1.call-done = bf16[1,2048,1024]{2,1,0:T(8,128)(2,1)} async-done(((bf16[1,512,1024]{2,1,0:T(8,128)(2,1)}), bf16[1,2048,1024]{2,1,0:T(8,128)(2,1)}) %all-gather.18.cloned.1.call-update) | async-done | bytes 4194320 | tf_op jit(solution)/shard_map/all_gather | solution.py:207
  183.2 6.0 multiply_reduce_fusion.19
  190.8 52.2 %all-gather.14.cloned.1.call-done = bf16[1024,2336]{0,1:T(8,128)(2,1)} async-done(((bf16[256,2336]{0,1:T(8,128)(2,1)}), bf16[1024,2336]{0,1:T(8,128)(2,1)}) %all-gather.14.cloned.1.call-update) | async-done | bytes 4784144 | tf_op jit(solution)/shard_map/all_gather | solution.py:207
  243.0 4.6 fusion.266
  255.7 6.8 fusion.50
  267.0 5.9 reshape.493
  297.3 9.6 multiply_reduce_fusion.14
  313.6 38.1 %all-gather.20.cloned.1.call-done = bf16[1,2048,1024]{2,1,0:T(8,128)(2,1)} async-done(((bf16[1,512,1024]{2,1,0:T(8,128)(2,1)}), bf16[1,2048,1024]{2,1,0:T(8,128)(2,1)}) %all-gather.20.cloned.1.call-update) | async-done | bytes 4194320 | tf_op jit(solution)/shard_map/all_gather | solution.py:207
  351.7 7.4 multiply_reduce_fusion.2
  359.2 7.1 multiply_reduce_fusion.3
  366.3 5.9 reshape.499
  375.6 20.6 %shard_map.196 = f32[32,64,128]{2,1,0:T(8,128)S(1)} custom-call(f32[32,1,128]{2,1,0:T(1,128)S(1)} %broadcast_in_dim.60.decay_ref, f32[32,64,128]{2,1,0:T(8,128)S(1)} %fusion.168.local_ref), custom_call_target="tpu_custom_call" | custom-call | flops 1048576 | bytes 33554432 | tf_op jit(solution)/shard_map/pallas_call | solution.py:90
  405.2 12.1 %multiply_reduce_fusion.10 = (f32[2,256,32]{1,2,0:T(8,128)S(1)}, f32[2,256,32]{1,2,0:T(8,128)S(1)}, f32[2,256,32,64]{1,3,2,0:T(8,128)}) fusion(f32[2,256,32,64]{1,3,2,0:T(8,128)} %fusion.143, f32[2,256,32,64]{1,0,3,2:T(2,128)} %reshape.493, f32[2,256,32]{1,2,0:T(8,128)S(1)} %bitcast.453, f32[2,256,32,64]{1,0,3,2:T(2,128)} %reshape.499, ...), kind=kOutput, calls=%fused_computation.132 | convolution fusion | flops 559906816 | bytes 17694848 | tf_op jit(solution)/shard_map/transpose(jvp(khij,kjhp->kihp))/dot_general | solution.py:157
  424.3 11.3 fusion.11
  453.0 9.2 fusion.40
  472.7 10.7 pad_add_fusion.1
  485.5 45.2 %all-reduce.38.cloned.1.call-done = bf16[512,1024]{1,0:T(8,128)(2,1)} async-done(((bf16[512,1024]{1,0:T(8,128)(2,1)}), bf16[512,1024]{1,0:T(8,128)(2,1)}) %all-reduce.38.cloned.1.call-update) | async-done | bytes 1048592 | tf_op jit(solution)/shard_map/psum | solution.py:267
  536.2 4.8 convolution_convert_fusion.1
  541.1 5.3 fusion.273
  546.5 5.9 multiply_reduce_fusion.16
  565.6 7.6 multiply_reduce_fusion.4
  573.2 5.0 multiply_reduce_fusion.5
  578.2 5.9 reshape.506
  587.3 17.8 %shard_map.197 = f32[32,64,128]{2,1,0:T(8,128)S(1)} custom-call(f32[32,1,128]{2,1,0:T(1,128)S(1)} %copy-done.3, f32[32,64,128]{2,1,0:T(8,128)S(1)} %fusion.167.local_ref), custom_call_target="tpu_custom_call" | custom-call | flops 1048576 | bytes 33554432 | tf_op jit(solution)/shard_map/pallas_call | solution.py:90
  606.6 43.7 %reduce-scatter.11.cloned.1.call-done = bf16[256,2336]{0,1:T(8,128)(2,1)} async-done(((bf16[1024,2336]{0,1:T(8,128)(2,1)}), bf16[256,2336]{0,1:T(8,128)(2,1)}) %reduce-scatter.11.cloned.1.call-update) | async-done | bytes 1196048 | tf_op jit(solution)/shard_map/reduce_scatter | solution.py:262
  658.5 12.3 %multiply_reduce_fusion.6 = (f32[2,256,32]{1,2,0:T(8,128)S(1)}, f32[2,256,32]{1,2,0:T(8,128)S(1)}, f32[2,256,32,64]{1,3,2,0:T(8,128)}) fusion(f32[2,256,32,64]{1,3,2,0:T(8,128)} %fusion.144, f32[2,256,32,64]{1,0,3,2:T(2,128)} %reshape.487, f32[2,256,32]{1,2,0:T(8,128)S(1)} %bitcast.448, f32[2,256,32,64]{1,0,3,2:T(2,128)} %reshape.506, f32[32]{0:T(128)} %mul.963, ...), kind=kOutput, calls=%fused_computation.127 | convolution fusion | flops 559906816 | bytes 17694848 | tf_op jit(solution)/shard_map/transpose(jvp(khij,kjhp->kihp))/dot_general | solution.py:157
  673.7 4.8 multiply_reduce_fusion.7
  680.0 11.2 fusion.13
  703.1 14.8 %fusion.44 = (f32[2304]{0:T(1024)S(1)}, f32[2304]{0:T(1024)S(1)}, f32[2304]{0:T(1024)S(1)}, f32[2304]{0:T(1024)S(1)}, f32[2304]{0:T(1024)S(1)}, /*index=5*/bf16[512,2304]{0,1:T(8,128)(2,1)S(1)}) fusion(f32[515,2304]{0,1:T(8,128)} %fusion.101, f32[512,2304]{0,1:T(8,128)} %get-tuple-element.100, f32[512,2048]{0,1:T(8,128)} %bitcast.425, ...), kind=kLoop, calls=%fused_computation.82 | loop fusion | flops 25940736 | bytes 30716928 | tf_op jit(solution)/shard_map/reduce_sum | solution.py:323
  728.6 10.5 pad_add_fusion
  740.6 26.9 %all-reduce.42.cloned.1.call-done = bf16[256,2336]{0,1:T(8,128)(2,1)} async-done(((bf16[256,2336]{0,1:T(8,128)(2,1)}), bf16[256,2336]{0,1:T(8,128)(2,1)}) %all-reduce.42.cloned.1.call-update) | async-done | bytes 1196048 | tf_op jit(solution)/shard_map/psum | solution.py:267
  772.9 4.9 convolution_convert_fusion
  779.6 7.2 add_bitcast_fusion
  788.1 5.6 fusion.274
  793.7 7.0 multiply_reduce_fusion.17
  800.7 22.5 %reduce-scatter.7.cloned.1.call-done = bf16[256,2048]{1,0:T(8,128)(2,1)} async-done(((bf16[1024,2048]{1,0:T(8,128)(2,1)}), bf16[256,2048]{1,0:T(8,128)(2,1)}) %reduce-scatter.7.cloned.1.call-update) | async-done | bytes 1048592 | tf_op jit(solution)/shard_map/reduce_scatter | solution.py:262
  823.3 61.1 %all-reduce.44.cloned.1.call-done = bf16[512,1024]{1,0:T(8,128)(2,1)} async-done(((bf16[512,1024]{1,0:T(8,128)(2,1)}), bf16[512,1024]{1,0:T(8,128)(2,1)}) %all-reduce.44.cloned.1.call-update) | async-done | bytes 1048592 | tf_op jit(solution)/shard_map/psum | solution.py:267
  889.5 54.9 %reduce-scatter.17.cloned.1.call-done = bf16[256,2336]{0,1:T(8,128)(2,1)} async-done(((bf16[1024,2336]{0,1:T(8,128)(2,1)}), bf16[256,2336]{0,1:T(8,128)(2,1)}) %reduce-scatter.17.cloned.1.call-update) | async-done | bytes 1196048 | tf_op jit(solution)/shard_map/reduce_scatter | solution.py:262
  944.4 61.0 %all-reduce.46.cloned.1.call-done = bf16[256,2048]{1,0:T(8,128)(2,1)} async-done(((bf16[256,2048]{1,0:T(8,128)(2,1)}), bf16[256,2048]{1,0:T(8,128)(2,1)}) %all-reduce.46.cloned.1.call-update) | async-done | bytes 1048592 | tf_op jit(solution)/shard_map/psum | solution.py:267
  1005.5 126.3 %all-reduce.36.cloned.1.call-done = f32[4,2,3672]{2,1,0:T(2,128)} async-done(((f32[4,2,3672]{2,1,0:T(2,128)}), f32[4,2,3672]{2,1,0:T(2,128)}) %all-reduce.36.cloned.1.call-update) | async-done | bytes 117520 | tf_op jit(solution)/shard_map/psum | solution.py:358
  1141.1 52.0 %all-reduce.48.cloned.1.call-done = bf16[1,256,2336]{1,2,0:T(8,128)(2,1)} async-done(((bf16[1,256,2336]{1,2,0:T(8,128)(2,1)}), bf16[1,256,2336]{1,2,0:T(8,128)(2,1)}) %all-reduce.48.cloned.1.call-update) | async-done | bytes 1196048 | tf_op jit(solution)/shard_map/psum | solution.py:267
  1193.2 4.9 maximum_convert_fusion
  (684 shorter events, 233.9 us)
Async XLA Ops:
  7.2 66.4 %all-gather.10.cloned.1.call-start = ((), (), s32[]{:S(2)}) async-start(), calls=%async_computation.6 | async-start | bytes 5980160 | tf_op jit(solution)/shard_map/all_gather | solution.py:207
  12.3 115.7 %all-gather.12.cloned.1.call-start = ((), (), s32[]{:S(2)}) async-start(), calls=%async_computation.7 | async-start | bytes 5242880 | tf_op jit(solution)/shard_map/all_gather | solution.py:207
  13.4 169.8 %all-gather.18.cloned.1.call-start = ((), (), s32[]{:S(2)}) async-start(), calls=%async_computation.23 | async-start | bytes 5242880 | tf_op jit(solution)/shard_map/all_gather | solution.py:207
  16.6 226.4 %all-gather.14.cloned.1.call-start = ((), (), s32[]{:S(2)}) async-start(), calls=%async_computation.8 | async-start | bytes 5980160 | tf_op jit(solution)/shard_map/all_gather | solution.py:207
  19.2 278.1 %all-gather.16.cloned.1.call-start = ((), (), s32[]{:S(2)}) async-start(), calls=%async_computation.9 | async-start | bytes 5242880 | tf_op jit(solution)/shard_map/all_gather | solution.py:207
  21.5 330.2 %all-gather.20.cloned.1.call-start = ((), (), s32[]{:S(2)}) async-start(), calls=%async_computation.24 | async-start | bytes 5242880 | tf_op jit(solution)/shard_map/all_gather | solution.py:207
  22.1 450.5 %reduce-scatter.15.cloned.1.call-start = ((), (), s32[]{:S(2)}) async-start(), calls=%async_computation.15 | async-start | bytes 5242880 | tf_op jit(solution)/shard_map/reduce_scatter | solution.py:262
  34.0 44.2 %copy-start.143 = (f32[4,1,256]{2,1,0:T(1,128)}, f32[4,1,256]{2,1,0:T(1,128)S(1)}, u32[]{:S(2)}) copy-start(f32[4,1,256]{2,1,0:T(1,128)S(1)} %get-tuple-element.130) | copy-start | bytes 12292
  34.0 155.2 %copy-start.145 = (f32[4,1,256]{2,1,0:T(1,128)}, f32[4,1,256]{2,1,0:T(1,128)S(1)}, u32[]{:S(2)}) copy-start(f32[4,1,256]{2,1,0:T(1,128)S(1)} %get-tuple-element.129) | copy-start | bytes 12292
  35.0 77.2 %copy-start.133 = (pred[256,256]{1,0:T(8,128)(4,1)}, pred[256,256]{1,0:T(8,128)(4,1)S(1)}, u32[]{:S(2)}) copy-start(pred[256,256]{1,0:T(8,128)(4,1)S(1)} %iota_compare_fusion) | copy-start | bytes 196612
  35.7 147.5 %copy-start.155 = (f32[4,1,512]{2,1,0:T(1,128)}, f32[4,1,512]{2,1,0:T(1,128)S(1)}, u32[]{:S(2)}) copy-start(f32[4,1,512]{2,1,0:T(1,128)S(1)} %get-tuple-element.128) | copy-start | bytes 24580
  36.0 42.2 %copy-start.159 = (f32[512]{0:T(512)}, f32[512]{0:T(512)S(1)}, u32[]{:S(2)}) copy-start(f32[512]{0:T(512)S(1)} %fusion.221) | copy-start | bytes 6148
  36.3 50.0 %copy-start.117 = (f32[2304]{0:T(1024)}, f32[2304]{0:T(1024)S(1)}, u32[]{:S(2)}) copy-start(f32[2304]{0:T(1024)S(1)} %mul.933) | copy-start | bytes 27652
  36.4 49.9 %copy-start.119 = (f32[2304]{0:T(1024)}, f32[2304]{0:T(1024)S(1)}, u32[]{:S(2)}) copy-start(f32[2304]{0:T(1024)S(1)} %mul.930) | copy-start | bytes 27652
  36.5 49.9 %copy-start.121 = (f32[2304]{0:T(1024)}, f32[2304]{0:T(1024)S(1)}, u32[]{:S(2)}) copy-start(f32[2304]{0:T(1024)S(1)} %mul.927) | copy-start | bytes 27652
  36.5 49.8 %copy-start.123 = (f32[2304]{0:T(1024)}, f32[2304]{0:T(1024)S(1)}, u32[]{:S(2)}) copy-start(f32[2304]{0:T(1024)S(1)} %mul.918) | copy-start | bytes 27652
  36.7 41.5 %copy-start.183 = (f32[32]{0:T(128)}, f32[32]{0:T(128)S(1)}, u32[]{:S(2)}) copy-start(f32[32]{0:T(128)S(1)} %neg.77) | copy-start | bytes 388
  37.7 217.9 %copy-start.125 = (f32[2304]{0:T(1024)}, f32[2304]{0:T(1024)S(1)}, u32[]{:S(2)}) copy-start(f32[2304]{0:T(1024)S(1)} %mul.989) | copy-start | bytes 27652
  37.8 217.9 %copy-start.127 = (f32[2304]{0:T(1024)}, f32[2304]{0:T(1024)S(1)}, u32[]{:S(2)}) copy-start(f32[2304]{0:T(1024)S(1)} %mul.986) | copy-start | bytes 27652
  37.9 217.8 %copy-start.129 = (f32[2304]{0:T(1024)}, f32[2304]{0:T(1024)S(1)}, u32[]{:S(2)}) copy-start(f32[2304]{0:T(1024)S(1)} %mul.983) | copy-start | bytes 27652
  38.0 217.7 %copy-start.131 = (f32[2304]{0:T(1024)}, f32[2304]{0:T(1024)S(1)}, u32[]{:S(2)}) copy-start(f32[2304]{0:T(1024)S(1)} %mul.974) | copy-start | bytes 27652
  81.7 4.3 collective-permute-start
  128.1 55.2 %copy-start.25 = (f32[1,512,1024]{2,1,0:T(8,128)S(1)}, f32[1,512,1024]{2,1,0:T(8,128)}, u32[]{:S(2)}) copy-start(f32[1,512,1024]{2,1,0:T(8,128)} %param.12) | copy-start | bytes 6291460
  138.8 50.4 %copy-start.171 = (f32[512]{0:T(512)}, f32[512]{0:T(512)S(1)}, u32[]{:S(2)}) copy-start(f32[512]{0:T(512)S(1)} %get-tuple-element.95) | copy-start | bytes 6148
  138.8 50.4 %copy-start.167 = (f32[512]{0:T(512)}, f32[512]{0:T(512)S(1)}, u32[]{:S(2)}) copy-start(f32[512]{0:T(512)S(1)} %fusion.222) | copy-start | bytes 6148
  189.2 58.3 %copy-start.173 = (f32[512]{0:T(512)}, f32[512]{0:T(512)S(1)}, u32[]{:S(2)}) copy-start(f32[512]{0:T(512)S(1)} %get-tuple-element.153) | copy-start | bytes 6148
  189.3 58.3 %copy-start.161 = (f32[512]{0:T(512)}, f32[512]{0:T(512)S(1)}, u32[]{:S(2)}) copy-start(f32[512]{0:T(512)S(1)} %fusion.223) | copy-start | bytes 6148
  190.8 56.8 %copy-start.87 = (bf16[512,1024]{1,0:T(8,128)(2,1)}, bf16[512,1024]{1,0:T(8,128)(2,1)S(1)}, u32[]{:S(2)}) copy-start(bf16[512,1024]{1,0:T(8,128)(2,1)S(1)} %multiply_convert_fusion.2) | copy-start | bytes 3145732
  249.0 123.2 %copy-start.95 = (f32[2,256,32]{1,2,0:T(8,128)}, f32[2,256,32]{1,2,0:T(8,128)S(1)}, u32[]{:S(2)}) copy-start(f32[2,256,32]{1,2,0:T(8,128)S(1)} %get-tuple-element.131) | copy-start | bytes 196612
  251.0 4.3 collective-permute-start.1
  313.5 171.9 %reduce-scatter.13.cloned.1.call-start = ((), (), s32[]{:S(2)}) async-start(), calls=%async_computation.14 | async-start | bytes 5242880 | tf_op jit(solution)/shard_map/reduce_scatter | solution.py:262
  404.3 126.4 %all-reduce.38.cloned.1.call-start = ((), (), s32[]{:S(2)}) async-start(), calls=%async_computation.16 | async-start | bytes 2097152 | tf_op jit(solution)/shard_map/psum | solution.py:267
  471.3 13.8 %collective-permute-start.2 = (f32[3,2304]{1,0:T(4,128)S(1)}, f32[3,2304]{1,0:T(4,128)S(1)}, u32[]{:S(2)}, u32[]{:S(2)}) collective-permute-start(f32[3,2304]{1,0:T(4,128)S(1)} %copy.303), channel_id=1, source_target_pairs={{1,0},{2,1},{3,2},{4,3},{5,4},{6,5},{7,6},{9,8},{10,9},{11,10},{12... | collective-permute-start | bytes 82952 | tf_op jit(solution)/shard_map/ppermute | solution.py:27
  472.7 133.9 %all-reduce.40.cloned.1.call-start = ((), (), s32[]{:S(2)}) async-start(), calls=%async_computation.17 | async-start | bytes 2097152 | tf_op jit(solution)/shard_map/psum | solution.py:267
  530.7 119.6 %reduce-scatter.11.cloned.1.call-start = ((), (), s32[]{:S(2)}) async-start(), calls=%async_computation.13 | async-start | bytes 5980160 | tf_op jit(solution)/shard_map/reduce_scatter | solution.py:262
  541.1 199.5 %reduce-scatter.9.cloned.1.call-start = ((), (), s32[]{:S(2)}) async-start(), calls=%async_computation.12 | async-start | bytes 5242880 | tf_op jit(solution)/shard_map/reduce_scatter | solution.py:262
  559.8 207.6 %all-reduce.42.cloned.1.call-start = ((), (), s32[]{:S(2)}) async-start(), calls=%async_computation.18 | async-start | bytes 2392064 | tf_op jit(solution)/shard_map/psum | solution.py:267
  587.3 63.1 %copy-start.68 = (bf16[2,256,128,1]{2,1,3,0:T(8,128)(2,1)S(1)}, bf16[2,256,128,1]{2,1,3,0:T(8,128)(2,1)}, u32[]{:S(2)}) copy-start(bf16[2,256,128,1]{2,1,3,0:T(8,128)(2,1)} %copy-done.67) | copy-start | bytes 393220
  650.3 172.9 %reduce-scatter.7.cloned.1.call-start = ((), (), s32[]{:S(2)}) async-start(), calls=%async_computation.11 | async-start | bytes 5242880 | tf_op jit(solution)/shard_map/reduce_scatter | solution.py:262
  657.6 226.8 %all-reduce.44.cloned.1.call-start = ((), (), s32[]{:S(2)}) async-start(), calls=%async_computation.19 | async-start | bytes 2097152 | tf_op jit(solution)/shard_map/psum | solution.py:267
  727.1 13.0 %collective-permute-start.3 = (f32[3,2304]{1,0:T(4,128)S(1)}, f32[3,2304]{1,0:T(4,128)S(1)}, u32[]{:S(2)}, u32[]{:S(2)}) collective-permute-start(f32[3,2304]{1,0:T(4,128)S(1)} %copy.326), channel_id=1, source_target_pairs={{1,0},{2,1},{3,2},{4,3},{5,4},{6,5},{7,6},{9,8},{10,9},{11,10},{12... | collective-permute-start | bytes 82952 | tf_op jit(solution)/shard_map/ppermute | solution.py:27
  767.5 176.9 %reduce-scatter.17.cloned.1.call-start = ((), (), s32[]{:S(2)}) async-start(), calls=%async_computation.21 | async-start | bytes 5980160 | tf_op jit(solution)/shard_map/reduce_scatter | solution.py:262
  777.9 227.5 %all-reduce.46.cloned.1.call-start = ((), (), s32[]{:S(2)}) async-start(), calls=%async_computation.20 | async-start | bytes 2097152 | tf_op jit(solution)/shard_map/psum | solution.py:267
  793.7 90.7 %copy-start.158 = (f32[512]{0:T(512)S(1)}, f32[512]{0:T(512)}, u32[]{:S(2)}) copy-start(f32[512]{0:T(512)} %copy-done.157) | copy-start | bytes 6148
  884.4 247.3 %all-reduce.36.cloned.1.call-start = ((), (), s32[]{:S(2)}) async-start(), calls=%async_computation.10 | async-start | bytes 237568 | tf_op jit(solution)/shard_map/psum | solution.py:358
  885.4 307.7 %all-reduce.48.cloned.1.call-start = ((), (), s32[]{:S(2)}) async-start(), calls=%async_computation.22 | async-start | bytes 2392064 | tf_op jit(solution)/shard_map/psum | solution.py:267
  1135.7 57.5 %copy-start.66 = (bf16[256,2336]{0,1:T(8,128)(2,1)S(1)}, bf16[256,2336]{0,1:T(8,128)(2,1)}, u32[]{:S(2)}) copy-start(bf16[256,2336]{0,1:T(8,128)(2,1)} %all-reduce.42.cloned.1.call-done) | copy-start | bytes 3588100
  1135.7 57.5 %copy-start.80 = (bf16[256,2048]{0,1:T(8,128)(2,1)S(1)}, bf16[256,2048]{0,1:T(8,128)(2,1)}, u32[]{:S(2)}) copy-start(bf16[256,2048]{0,1:T(8,128)(2,1)} %all-reduce.40.cloned.1.call-done) | copy-start | bytes 3145732
  (184 other events, 1393.2 us)
Sparse Core Ops, SparseCore 0:
  12.4 61.1 all-gather.9
  75.4 52.5 all-gather.11
  130.5 52.6 all-gather.17
  185.5 57.4 all-gather.13
  244.7 52.5 all-gather.15
  299.0 52.6 all-gather.19
  354.7 52.6 reduce-scatter.14
  410.6 52.6 reduce-scatter.12
  472.8 57.8 all-reduce.37
  532.9 57.7 all-reduce.39
  593.7 56.5 reduce-scatter.10
  653.1 52.6 reduce-scatter.8
  708.4 59.0 all-reduce.41
  770.5 52.6 reduce-scatter.6
  825.5 58.8 all-reduce.43
  887.8 56.5 reduce-scatter.16
  946.6 58.7 all-reduce.45
  1011.4 120.2 all-reduce.35
  1134.1 59.0 all-reduce.47
